TPU v7x, 512 devices: a whole 4x4x16 slice. The times are simulated.
512 devices in a mesh: seq: 16 (over x, y), dp: 32 (over z, core).
Axes of the slice: x: 4, y: 4, z: 16, core: 2. Of those that a mesh axis runs over, the one named last changes fastest.
Arguments:
- signal: bfloat16 [32, 4096, 128], P('dp', 'seq'), may hold values from -6 to 6
- out_grad: bfloat16 [32, 4096, 128], P('dp', 'seq'), may hold values from -6 to 6
- filt: float32 [4096, 128], P('seq'), may hold values from -1.1 to 1.1, as said below
- skip: float32 [128], replicated, may hold values from 0.5 to 1.5
Outputs:
- in_grad: bfloat16 [32, 4096, 128], P('dp', 'seq')
- filt_grad: float32 [4096, 128], P(('seq', 'dp'))
Inputs may be any that keep to these rules, and one draw needn't show every extreme that they name: `filt`: each channel's filter is an independent real sequence.
All inputs are finite; a program needn't handle non-finite values.
Results may differ from a plain program's by a relative error of at most 0.001.
Values may be sent and summed in bfloat16 or wider, within the bound.
A program may use at most 64 MiB of HBM per device.

v0:
```python
import functools
import math

import jax
import jax.numpy as jnp
import ml_dtypes
import numpy as np
from jax import lax
from jax.experimental import pallas as pl
from jax.experimental.pallas import tpu as pltpu
from jax.sharding import PartitionSpec as P

SEQ, ZED, CORES = 16, 16, 2
PANEL, HALF, CH, OWN = 256, 128, 128, 8
FREQ = PANEL
F32, BF16 = jnp.float32, jnp.bfloat16
NT = (((1,), (1,)), ((), ()))
NN = (((1,), (0,)), ((), ()))


def table():
    product = np.arange(PANEL)[:, None] * (2 * np.arange(FREQ)[None, :] + 1) % (4 * PANEL)
    phase = 2.0 * math.pi / (4 * PANEL) * product.astype(np.float64)
    full = np.concatenate([np.cos(phase), -np.sin(phase)], axis=1)
    high = full.astype(ml_dtypes.bfloat16)
    rest = (full - high.astype(np.float64)).astype(ml_dtypes.bfloat16)
    return np.stack([high, rest])


def dot(a, b, dims):
    return lax.dot_general(a, b, dims, preferred_element_type=F32)


def split(x):
    high = x.astype(BF16)
    return high, (x - high.astype(F32)).astype(BF16)


def correlate(x_of, g_ref, v_ref):
    for lane in range(0, FREQ, HALF):
        total_re = total_im = None
        for a in range(SEQ):
            x_re, x_im = x_of(a, lane)
            g_re = g_ref[a:, :, lane : lane + HALF]
            g_im = g_ref[a:, :, FREQ + lane : FREQ + lane + HALF]
            new_re = x_re * g_re + x_im * g_im
            new_im = x_re * g_im - x_im * g_re
            if a == 0:
                total_re, total_im = new_re, new_im
            else:
                n = SEQ - a
                total_re = jnp.concatenate([total_re[:n] + new_re, total_re[n:]], axis=0)
                total_im = jnp.concatenate([total_im[:n] + new_im, total_im[n:]], axis=0)
        for total, first in ((total_re, lane), (total_im, FREQ + lane)):
            high, rest = split(total.reshape(SEQ * OWN, HALF))
            v_ref[0 : SEQ * OWN, first : first + HALF] = high
            v_ref[SEQ * OWN :, first : first + HALF] = rest


def kernel(
    u_ref, g_ref, f_ref, skip_ref, w_ref, in_ref, fg_ref,
    send_ug, recv_ug, send_f, recv_f, spec, spec_f, spin, v_ref, part, from_core, pair_sum, recv_z,
    own_sum, recv_s, send_in, recv_in, send_sem, recv_sem,
):
    me, dp = lax.axis_index("seq"), lax.axis_index("dp")
    z, core = lax.div(dp, CORES), lax.rem(dp, CORES)
    seq_peer = lambda k: lax.rem(me + k, SEQ)
    z_peer = lambda k: lax.rem(z + k, ZED)
    other = 1 - core

    barrier = pltpu.get_barrier_semaphore()
    for k in range(1, SEQ):
        pl.semaphore_signal(barrier, inc=1, device_id={"seq": seq_peer(k)})
    for k in range(1, ZED):
        pl.semaphore_signal(barrier, inc=1, device_id={"dp": z_peer(k) * CORES + core})
    pl.semaphore_signal(barrier, inc=1, device_id={"dp": z * CORES + other})

    def send(src, dst, place, device):
        pltpu.make_async_remote_copy(
            src_ref=src, dst_ref=dst, send_sem=send_sem.at[place], recv_sem=recv_sem.at[place], device_id=device
        ).start()

    def await_bytes(ref, sem, place):
        pltpu.make_async_copy(ref, ref, sem.at[place]).wait()

    rows = lax.broadcasted_iota(jnp.int32, (CH, CH), 0)
    eye = (rows == lax.broadcasted_iota(jnp.int32, (CH, CH), 1)).astype(F32).astype(BF16)

    def stage(first, second, out_ref):
        first, second = dot(eye, first, NT), dot(eye, second, NT)
        for h in range(2):
            lanes = slice(h * HALF, (h + 1) * HALF)
            tile = jnp.concatenate(
                [first[:, lanes].reshape(SEQ, OWN, HALF), second[:, lanes].reshape(SEQ, OWN, HALF)], axis=1
            )
            out_ref[:, h] = tile.astype(BF16)

    stage(u_ref[0], g_ref[0], send_ug)
    tap = lax.broadcasted_iota(jnp.int32, (PANEL, CH), 0) + me
    filt = f_ref[...] + jnp.where(tap == 0, jnp.broadcast_to(skip_ref[...], (PANEL, CH)), 0.0)
    stage(*split(filt), send_f)

    pl.semaphore_wait(barrier, SEQ + ZED - 1)
    for k in range(1, SEQ):
        peer = seq_peer(k)
        send(send_ug.at[peer], recv_ug.at[me], 0, {"seq": peer})
    for k in range(1, SEQ):
        peer = seq_peer(k)
        send(send_f.at[peer], recv_f.at[me], 1, {"seq": peer})
    recv_ug[me] = send_ug[me]
    recv_f[me] = send_f[me]

    def transform(tiles_ref):
        lhs = jnp.concatenate(
            [tiles_ref[:, 0].reshape(2 * SEQ * OWN, HALF), tiles_ref[:, 1].reshape(2 * SEQ * OWN, HALF)], axis=1
        )
        return dot(lhs, w_ref[0], NN) + dot(lhs, w_ref[1], NN)

    await_bytes(recv_ug.at[pl.ds(0, SEQ - 1)], recv_sem, 0)
    spec[...] = transform(recv_ug).reshape(SEQ, 2, OWN, 2 * FREQ)

    lanes = lax.broadcasted_iota(jnp.int32, (OWN, FREQ), 1)
    sign = 1.0 - 2.0 * lax.rem(lanes, 2).astype(F32)
    for a in range(SEQ):
        re, im = spec[a, 1, :, :FREQ], spec[a, 1, :, FREQ:]
        if a < SEQ - 1:
            re, im = re + sign * spec[a + 1, 1, :, FREQ:], im - sign * spec[a + 1, 1, :, :FREQ]
        spin[a, :, :FREQ] = re
        spin[a, :, FREQ:] = im

    correlate(
        lambda a, lane: (
            spec[a, 0, :, lane : lane + HALF], spec[a, 0, :, FREQ + lane : FREQ + lane + HALF]
        ),
        spin, v_ref,
    )
    wide = dot(w_ref[0], v_ref[...], NT)
    weight = wide[:, :CH] + wide[:, CH:] + dot(w_ref[1], v_ref[0 : SEQ * OWN], NT)
    weight = weight * (1.0 / (PANEL * math.sqrt(CORES * ZED * SEQ * PANEL)))
    weight = weight.reshape(ZED, CORES, OWN, CH)
    for side in range(CORES):
        part[side] = weight[:, side]
    send(part.at[other], from_core, 2, {"dp": z * CORES + other})

    await_bytes(recv_f.at[pl.ds(0, SEQ - 1)], recv_sem, 1)
    both = transform(recv_f).reshape(SEQ, 2, OWN, 2 * FREQ)
    spec_f[...] = both[:, 0] + both[:, 1]

    await_bytes(from_core, recv_sem, 2)
    pair_sum[...] = part[core] + from_core[...]
    for k in range(1, ZED):
        peer = z_peer(k)
        send(pair_sum.at[peer], recv_z.at[z], 3, {"dp": peer * CORES + core})
    recv_z[z] = pair_sum[z]

    correlate(
        lambda a, lane: (spec_f[a, :, lane : lane + HALF], spec_f[a, :, FREQ + lane : FREQ + lane + HALF]),
        spin, v_ref,
    )
    tall = dot(v_ref[...], w_ref[0], NT)
    back = tall[: SEQ * OWN] + tall[SEQ * OWN :] + dot(v_ref[0 : SEQ * OWN], w_ref[1], NT)
    back = (back * (1.0 / PANEL)).reshape(SEQ, OWN, PANEL)
    send_in[...] = jnp.concatenate([back[:, :, :HALF], back[:, :, HALF:]], axis=1).astype(BF16)
    for k in range(1, SEQ):
        peer = seq_peer(k)
        send(send_in.at[peer], recv_in.at[me], 4, {"seq": peer})
    recv_in[me] = send_in[me]

    await_bytes(recv_z.at[pl.ds(0, ZED - 1)], recv_sem, 3)
    own_sum[...] = jnp.sum(recv_z[...], axis=0)
    for k in range(1, SEQ):
        send(own_sum, recv_s.at[me], 5, {"seq": seq_peer(k)})
    recv_s[me] = own_sum[...]

    await_bytes(recv_in.at[pl.ds(0, SEQ - 1)], recv_sem, 4)
    for h in range(2):
        block = recv_in[...].astype(F32)[:, h * OWN : (h + 1) * OWN].reshape(CH, HALF)
        in_ref[0, h * HALF : (h + 1) * HALF] = block.T.astype(BF16)

    await_bytes(recv_s.at[pl.ds(0, SEQ - 1)], recv_sem, 5)
    group = lax.div(lax.broadcasted_iota(jnp.int32, (OWN, CH), 1), OWN)
    result = jnp.zeros((OWN, CH), F32)
    for s in range(SEQ):
        turned = pltpu.roll(recv_s[s], lax.rem(s + SEQ - me, SEQ) * OWN, 1)
        result = jnp.where(group == s, turned, result)
    fg_ref[...] = result

    await_bytes(send_ug.at[pl.ds(0, SEQ - 1)], send_sem, 0)
    await_bytes(send_f.at[pl.ds(0, SEQ - 1)], send_sem, 1)
    await_bytes(from_core, send_sem, 2)
    await_bytes(pair_sum.at[pl.ds(0, ZED - 1)], send_sem, 3)
    await_bytes(send_in.at[pl.ds(0, SEQ - 1)], send_sem, 4)
    await_bytes(recv_s.at[pl.ds(0, SEQ - 1)], send_sem, 5)


def on_device(signal, out_grad, filt, skip):
    vmem = pl.BlockSpec(memory_space=pltpu.VMEM)
    tiles = (SEQ, 2, 2 * OWN, HALF)
    return pl.pallas_call(
        kernel,
        out_shape=(
            jax.ShapeDtypeStruct((1, PANEL, CH), BF16),
            jax.ShapeDtypeStruct((OWN, CH), F32),
        ),
        in_specs=[vmem] * 5,
        out_specs=(vmem, vmem),
        scratch_shapes=[
            pltpu.VMEM(tiles, BF16),
            pltpu.VMEM(tiles, BF16),
            pltpu.VMEM(tiles, BF16),
            pltpu.VMEM(tiles, BF16),
            pltpu.VMEM((SEQ, 2, OWN, 2 * FREQ), F32),
            pltpu.VMEM((SEQ, OWN, 2 * FREQ), F32),
            pltpu.VMEM((SEQ, OWN, 2 * FREQ), F32),
            pltpu.VMEM((2 * SEQ * OWN, 2 * FREQ), BF16),
            pltpu.VMEM((CORES, ZED, OWN, CH), F32),
            pltpu.VMEM((ZED, OWN, CH), F32),
            pltpu.VMEM((ZED, OWN, CH), F32),
            pltpu.VMEM((ZED, OWN, CH), F32),
            pltpu.VMEM((OWN, CH), F32),
            pltpu.VMEM((SEQ, OWN, CH), F32),
            pltpu.VMEM((SEQ, 2 * OWN, HALF), BF16),
            pltpu.VMEM((SEQ, 2 * OWN, HALF), BF16),
            pltpu.SemaphoreType.DMA((6,)),
            pltpu.SemaphoreType.DMA((6,)),
        ],
        compiler_params=pltpu.CompilerParams(
            collective_id=0, has_side_effects=True, vmem_limit_bytes=32 * 1024 * 1024
        ),
    )(signal, out_grad, filt, skip.reshape(1, CH), jnp.asarray(table()))


def solution(mesh):
    placed = (P("dp", "seq", None), P("dp", "seq", None), P("seq", None), P())
    return jax.shard_map(
        on_device,
        mesh=mesh,
        in_specs=placed,
        out_specs=(P("dp", "seq", None), P(("seq", "dp"), None)),
        check_vma=False,
    )
```

profile of v0, /device:TPU:1, one launch (start us, length us, event | category | flops | bytes accessed | tf_op | source)
XLA Modules:
  0.0 41.6 jit_solution(8048656712849780676)
XLA Ops:
  0.6 0.0 copy-start.4
  0.6 0.6 %copy-done.4 = f32[128]{0:T(128)S(1)} copy-done((f32[128]{0:T(128)S(1)}, f32[128]{0:T(128)}, u32[]{:S(2)}) %copy-start.4) | copy-done | bytes 536
  1.3 0.0 copy-start
  1.3 1.0 %copy-done = bf16[2,256,512]{2,1,0:T(8,128)(2,1)S(1)} copy-done((bf16[2,256,512]{2,1,0:T(8,128)(2,1)S(1)}, bf16[2,256,512]{2,1,0:T(8,128)(2,1)}, u32[]{:S(2)}) %copy-start) | copy-done | bytes 524312
  2.3 0.0 copy-start.1
  2.3 0.9 %copy-done.1 = f32[256,128]{1,0:T(8,128)S(1)} copy-done((f32[256,128]{1,0:T(8,128)S(1)}, f32[256,128]{1,0:T(8,128)}, u32[]{:S(2)}) %copy-start.1) | copy-done | bytes 131096
  3.2 0.0 copy-start.2
  3.2 0.8 %copy-done.2 = bf16[1,256,128]{2,1,0:T(8,128)(2,1)S(1)} copy-done((bf16[1,256,128]{2,1,0:T(8,128)(2,1)S(1)}, bf16[1,256,128]{2,1,0:T(8,128)(2,1)}, u32[]{:S(2)}) %copy-start.2) | copy-done | bytes 65560
  4.1 0.0 copy-start.3
  4.1 0.8 %copy-done.3 = bf16[1,256,128]{2,1,0:T(8,128)(2,1)S(1)} copy-done((bf16[1,256,128]{2,1,0:T(8,128)(2,1)S(1)}, bf16[1,256,128]{2,1,0:T(8,128)(2,1)}, u32[]{:S(2)}) %copy-start.3) | copy-done | bytes 65560
  4.9 35.5 %shard_map.68 = (bf16[1,256,128]{2,1,0:T(8,128)(2,1)S(1)}, f32[8,128]{1,0:T(8,128)S(1)}) custom-call(bf16[1,256,128]{2,1,0:T(8,128)(2,1)S(1)} %copy-done.2, bf16[1,256,128]{2,1,0:T(8,128)(2,1)S(1)} %copy-done.3, f32[256,128]{1,0:T(8,128)S(1)} %copy-done.1, f32[1,128]{1,0:T(1,128)S(1)} %bitcast.1, bf16[2,256,512]{2,1,0:T(8,128)(2,1)S(1)} %copy-done), custom_call_target="tpu_custom_call" | custom-call | tf_op jit(solution)/shard_map/pallas_call | solution.py:199
  40.4 0.6 %copy.9 = bf16[1,256,128]{2,1,0:T(8,128)(2,1)} copy(bf16[1,256,128]{2,1,0:T(8,128)(2,1)S(1)} %get-tuple-element.4) | data formatting | bytes 131072
  41.0 0.6 %copy.10 = f32[8,128]{1,0:T(8,128)} copy(f32[8,128]{1,0:T(8,128)S(1)} %get-tuple-element.5) | data formatting | bytes 8192
Async XLA Ops:
  0.6 0.7 %copy-start.4 = (f32[128]{0:T(128)S(1)}, f32[128]{0:T(128)}, u32[]{:S(2)}) copy-start(f32[128]{0:T(128)} %param.8) | copy-start | bytes 1540
  1.3 1.0 %copy-start = (bf16[2,256,512]{2,1,0:T(8,128)(2,1)S(1)}, bf16[2,256,512]{2,1,0:T(8,128)(2,1)}, u32[]{:S(2)}) copy-start(bf16[2,256,512]{2,1,0:T(8,128)(2,1)} %constant.2.clone.w_ref) | copy-start | bytes 1572868
  2.3 0.9 %copy-start.1 = (f32[256,128]{1,0:T(8,128)S(1)}, f32[256,128]{1,0:T(8,128)}, u32[]{:S(2)}) copy-start(f32[256,128]{1,0:T(8,128)} %f_ref.1) | copy-start | bytes 393220
  3.2 0.8 %copy-start.2 = (bf16[1,256,128]{2,1,0:T(8,128)(2,1)S(1)}, bf16[1,256,128]{2,1,0:T(8,128)(2,1)}, u32[]{:S(2)}) copy-start(bf16[1,256,128]{2,1,0:T(8,128)(2,1)} %u_ref.1) | copy-start | bytes 196612
  4.1 0.8 %copy-start.3 = (bf16[1,256,128]{2,1,0:T(8,128)(2,1)S(1)}, bf16[1,256,128]{2,1,0:T(8,128)(2,1)}, u32[]{:S(2)}) copy-start(bf16[1,256,128]{2,1,0:T(8,128)(2,1)} %g_ref.1) | copy-start | bytes 196612
where the time goes:
time: 41.9 us; the launch traced here: 41.6 us
  Pallas kernels  35.5 us (85%)
  local copies, waits for them, and re-layouts  5.5 us (13%)
  between operations  0.65 us (2%)
    pallas_call x1, Pallas kernels, on_device(): pl.pallas_call(kernel, out_shape=(jax.ShapeDtypeStruct((1, PANEL, CH), BF...  35.5 us
    unnamed x12, local copies, waits for them, and re-layouts  5.5 us

commit v1 on v0

--- a/solution.py
+++ b/solution.py
@@ -13,6 +13,11 @@
 SEQ, ZED, CORES = 16, 16, 2
 PANEL, HALF, CH, OWN = 256, 128, 128, 8
 FREQ = PANEL
+NEAR = 4
+SEQ_OFFSETS = sorted(
+    ((i, j) for i in range(4) for j in range(4) if i + j), key=lambda o: -sum(min(k, 4 - k) for k in o)
+)
+Z_OFFSETS = sorted(range(1, ZED), key=lambda k: -min(k, ZED - k))
 F32, BF16 = jnp.float32, jnp.bfloat16
 NT = (((1,), (1,)), ((), ()))
 NN = (((1,), (0,)), ((), ()))
@@ -58,22 +63,34 @@
 
 
 def kernel(
-    u_ref, g_ref, f_ref, skip_ref, w_ref, in_ref, fg_ref,
-    send_ug, recv_ug, send_f, recv_f, spec, spec_f, spin, v_ref, part, from_core, pair_sum, recv_z,
-    own_sum, recv_s, send_in, recv_in, send_sem, recv_sem,
+    u_hbm, g_hbm, f_hbm, skip_hbm, w_hbm, in_ref, fg_ref,
+    u_ref, g_ref, f_ref, skip_ref, w_ref, send_ug, recv_ug, send_f, recv_f, spec, spec_f, spin, v_ref, part, from_core, pair_sum, recv_z,
+    own_sum, recv_s, send_in, recv_in, send_sem, recv_sem, load_sem, relay_sem,
 ):
     me, dp = lax.axis_index("seq"), lax.axis_index("dp")
     z, core = lax.div(dp, CORES), lax.rem(dp, CORES)
-    seq_peer = lambda k: lax.rem(me + k, SEQ)
+    x, y = lax.div(me, 4), lax.rem(me, 4)
+    seq_peers = [lax.rem(x + i, 4) * 4 + lax.rem(y + j, 4) for i, j in SEQ_OFFSETS]
     z_peer = lambda k: lax.rem(z + k, ZED)
     other = 1 - core
 
+    loads = [
+        pltpu.make_async_copy(src, dst, load_sem.at[i])
+        for i, (src, dst) in enumerate(
+            ((u_hbm, u_ref), (g_hbm, g_ref), (f_hbm, f_ref), (skip_hbm, skip_ref), (w_hbm, w_ref))
+        )
+    ]
+    for load in loads[:2]:
+        load.start()
     barrier = pltpu.get_barrier_semaphore()
-    for k in range(1, SEQ):
-        pl.semaphore_signal(barrier, inc=1, device_id={"seq": seq_peer(k)})
-    for k in range(1, ZED):
+    for k in Z_OFFSETS[-2 * NEAR :]:
         pl.semaphore_signal(barrier, inc=1, device_id={"dp": z_peer(k) * CORES + core})
+    for peer in seq_peers:
+        pl.semaphore_signal(barrier, inc=1, device_id={"seq": peer})
     pl.semaphore_signal(barrier, inc=1, device_id={"dp": z * CORES + other})
+
+    for load in loads[2:]:
+        load.start()
 
     def send(src, dst, place, device):
         pltpu.make_async_remote_copy(
@@ -95,20 +112,26 @@
             )
             out_ref[:, h] = tile.astype(BF16)
 
+    loads[0].wait()
+    loads[1].wait()
     stage(u_ref[0], g_ref[0], send_ug)
+    loads[2].wait()
+    loads[3].wait()
     tap = lax.broadcasted_iota(jnp.int32, (PANEL, CH), 0) + me
     filt = f_ref[...] + jnp.where(tap == 0, jnp.broadcast_to(skip_ref[...], (PANEL, CH)), 0.0)
     stage(*split(filt), send_f)
 
-    pl.semaphore_wait(barrier, SEQ + ZED - 1)
-    for k in range(1, SEQ):
-        peer = seq_peer(k)
+    pl.semaphore_wait(barrier, SEQ + 2 * NEAR)
+    for k in (NEAR, ZED - NEAR):
+        pl.semaphore_signal(relay_sem, inc=1, device_id={"dp": z_peer(k) * CORES + core})
+    for peer in seq_peers:
         send(send_ug.at[peer], recv_ug.at[me], 0, {"seq": peer})
-    for k in range(1, SEQ):
-        peer = seq_peer(k)
+    for peer in seq_peers:
         send(send_f.at[peer], recv_f.at[me], 1, {"seq": peer})
     recv_ug[me] = send_ug[me]
     recv_f[me] = send_f[me]
+
+    loads[4].wait()
 
     def transform(tiles_ref):
         lhs = jnp.concatenate(
@@ -148,7 +171,8 @@
 
     await_bytes(from_core, recv_sem, 2)
     pair_sum[...] = part[core] + from_core[...]
-    for k in range(1, ZED):
+    pl.semaphore_wait(relay_sem, 2)
+    for k in Z_OFFSETS:
         peer = z_peer(k)
         send(pair_sum.at[peer], recv_z.at[z], 3, {"dp": peer * CORES + core})
     recv_z[z] = pair_sum[z]
@@ -161,15 +185,14 @@
     back = tall[: SEQ * OWN] + tall[SEQ * OWN :] + dot(v_ref[0 : SEQ * OWN], w_ref[1], NT)
     back = (back * (1.0 / PANEL)).reshape(SEQ, OWN, PANEL)
     send_in[...] = jnp.concatenate([back[:, :, :HALF], back[:, :, HALF:]], axis=1).astype(BF16)
-    for k in range(1, SEQ):
-        peer = seq_peer(k)
+    for peer in seq_peers:
         send(send_in.at[peer], recv_in.at[me], 4, {"seq": peer})
     recv_in[me] = send_in[me]
 
     await_bytes(recv_z.at[pl.ds(0, ZED - 1)], recv_sem, 3)
     own_sum[...] = jnp.sum(recv_z[...], axis=0)
-    for k in range(1, SEQ):
-        send(own_sum, recv_s.at[me], 5, {"seq": seq_peer(k)})
+    for peer in seq_peers:
+        send(own_sum, recv_s.at[me], 5, {"seq": peer})
     recv_s[me] = own_sum[...]
 
     await_bytes(recv_in.at[pl.ds(0, SEQ - 1)], recv_sem, 4)
@@ -195,16 +218,22 @@
 
 def on_device(signal, out_grad, filt, skip):
     vmem = pl.BlockSpec(memory_space=pltpu.VMEM)
+    operands = (signal, out_grad, filt, skip.reshape(1, CH), jnp.asarray(table()))
     tiles = (SEQ, 2, 2 * OWN, HALF)
     return pl.pallas_call(
         kernel,
         out_shape=(
-            jax.ShapeDtypeStruct((1, PANEL, CH), BF16),
-            jax.ShapeDtypeStruct((OWN, CH), F32),
+            pltpu.VMEM((1, PANEL, CH), BF16),
+            pltpu.VMEM((OWN, CH), F32),
         ),
-        in_specs=[vmem] * 5,
+        in_specs=[pl.BlockSpec(memory_space=pltpu.HBM)] * 5,
         out_specs=(vmem, vmem),
         scratch_shapes=[
+            pltpu.VMEM((1, PANEL, CH), BF16),
+            pltpu.VMEM((1, PANEL, CH), BF16),
+            pltpu.VMEM((PANEL, CH), F32),
+            pltpu.VMEM((1, CH), F32),
+            pltpu.VMEM((2, PANEL, 2 * FREQ), BF16),
             pltpu.VMEM(tiles, BF16),
             pltpu.VMEM(tiles, BF16),
             pltpu.VMEM(tiles, BF16),
@@ -223,11 +252,13 @@
             pltpu.VMEM((SEQ, 2 * OWN, HALF), BF16),
             pltpu.SemaphoreType.DMA((6,)),
             pltpu.SemaphoreType.DMA((6,)),
+            pltpu.SemaphoreType.DMA((5,)),
+            pltpu.SemaphoreType.REGULAR,
         ],
         compiler_params=pltpu.CompilerParams(
-            collective_id=0, has_side_effects=True, vmem_limit_bytes=32 * 1024 * 1024
+            collective_id=0, has_side_effects=True, vmem_limit_bytes=16 * 1024 * 1024
         ),
-    )(signal, out_grad, filt, skip.reshape(1, CH), jnp.asarray(table()))
+    )(*(pltpu.with_memory_space_constraint(x, pltpu.HBM) for x in operands))
 
 
 def solution(mesh):

time: 41.9 us -> 36.4 us (0.87)
  local copies, waits for them, and re-layouts: 5.5 us -> 1.22 us
  Pallas kernels: 35.5 us -> 34.4 us
    unnamed x12 -> x2, local copies, waits for them, and re-layouts: 5.5 us -> 1.22 us
    pallas_call x1, Pallas kernels: 35.5 us -> 34.4 us  [on_device(): pl.pallas_call(kernel, out_shape=(pltpu.VMEM((1, PANEL, CH), BF16), pltpu...]
where the time goes in v1:
time: 36.4 us; the launch traced here: 36.2 us
  Pallas kernels  34.4 us (95%)
  local copies, waits for them, and re-layouts  1.22 us (3%)
  between operations  0.64 us (2%)
    pallas_call x1, Pallas kernels, on_device(): pl.pallas_call(kernel, out_shape=(pltpu.VMEM((1, PANEL, CH), BF16), pltpu...  34.4 us
    unnamed x2, local copies, waits for them, and re-layouts  1.22 us

profile of v1, /device:TPU:1, one launch (start us, length us, event | category | flops | bytes accessed | tf_op | source)
XLA Modules:
  0.0 36.2 jit_solution(5710353338049796969)
XLA Ops:
  0.6 34.4 %shard_map.68 = (bf16[1,256,128]{2,1,0:T(8,128)(2,1)S(1)}, f32[8,128]{1,0:T(8,128)S(1)}) custom-call(bf16[1,256,128]{2,1,0:T(8,128)(2,1)} %u_hbm.1, bf16[1,256,128]{2,1,0:T(8,128)(2,1)} %g_hbm.1, f32[256,128]{1,0:T(8,128)} %f_hbm.1, f32[1,128]{1,0:T(1,128)} %bitcast.1, bf16[2,256,512]{2,1,0:T(8,128)(2,1)} %constant.2.clone.w_hbm), custom_call_target="tpu_custom_call" | custom-call | tf_op jit(solution)/shard_map/pallas_call | solution.py:223
  35.0 0.6 %copy.9 = bf16[1,256,128]{2,1,0:T(8,128)(2,1)} copy(bf16[1,256,128]{2,1,0:T(8,128)(2,1)S(1)} %get-tuple-element.2) | data formatting | bytes 131072
  35.7 0.6 %copy.10 = f32[8,128]{1,0:T(8,128)} copy(f32[8,128]{1,0:T(8,128)S(1)} %get-tuple-element.3) | data formatting | bytes 8192

commit v2 on v1

--- a/solution.py
+++ b/solution.py
@@ -14,6 +14,7 @@
 PANEL, HALF, CH, OWN = 256, 128, 128, 8
 FREQ = PANEL
 NEAR = 4
+EARLY = (1,)
 SEQ_OFFSETS = sorted(
     ((i, j) for i in range(4) for j in range(4) if i + j), key=lambda o: -sum(min(k, 4 - k) for k in o)
 )
@@ -62,10 +63,15 @@
             v_ref[SEQ * OWN :, first : first + HALF] = rest
 
 
+def beside(dp, place):
+    near = min((dp // CORES - place // CORES) % ZED, (place // CORES - dp // CORES) % ZED)
+    return near == 0 or (near <= NEAR and dp % CORES == place % CORES)
+
+
 def kernel(
     u_hbm, g_hbm, f_hbm, skip_hbm, w_hbm, in_ref, fg_ref,
     u_ref, g_ref, f_ref, skip_ref, w_ref, send_ug, recv_ug, send_f, recv_f, spec, spec_f, spin, v_ref, part, from_core, pair_sum, recv_z,
-    own_sum, recv_s, send_in, recv_in, send_sem, recv_sem, load_sem, relay_sem,
+    own_sum, recv_s, send_in, recv_in, send_sem, recv_sem, load_sem, relay_sem, vouch_sem, early_row, recv_early,
 ):
     me, dp = lax.axis_index("seq"), lax.axis_index("dp")
     z, core = lax.div(dp, CORES), lax.rem(dp, CORES)
@@ -92,6 +98,20 @@
     for load in loads[2:]:
         load.start()
 
+    early_dp = (dp >= EARLY[0]) & (dp <= EARLY[-1])
+    early = (me == 0) & early_dp
+
+    greetings = SEQ + 2 * NEAR
+    for place in EARLY:
+        strangers = [k for k in range(CORES * ZED) if not beside(k, place)]
+        unknown = functools.reduce(jnp.logical_or, [dp == k for k in strangers])
+        greetings += jnp.where((me == 0) & unknown, 1, 0)
+
+        @pl.when((me == 0) & (dp == place))
+        def _():
+            for k in strangers:
+                pl.semaphore_signal(barrier, inc=1, device_id={"dp": k})
+
     def send(src, dst, place, device):
         pltpu.make_async_remote_copy(
             src_ref=src, dst_ref=dst, send_sem=send_sem.at[place], recv_sem=recv_sem.at[place], device_id=device
@@ -121,9 +141,15 @@
     filt = f_ref[...] + jnp.where(tap == 0, jnp.broadcast_to(skip_ref[...], (PANEL, CH)), 0.0)
     stage(*split(filt), send_f)
 
-    pl.semaphore_wait(barrier, SEQ + 2 * NEAR)
+    pl.semaphore_wait(barrier, greetings)
     for k in (NEAR, ZED - NEAR):
         pl.semaphore_signal(relay_sem, inc=1, device_id={"dp": z_peer(k) * CORES + core})
+
+    @pl.when(me == 0)
+    def _():
+        for peer in seq_peers:
+            pl.semaphore_signal(vouch_sem, inc=1, device_id={"seq": peer})
+
     for peer in seq_peers:
         send(send_ug.at[peer], recv_ug.at[me], 0, {"seq": peer})
     for peer in seq_peers:
@@ -160,6 +186,30 @@
     wide = dot(w_ref[0], v_ref[...], NT)
     weight = wide[:, :CH] + wide[:, CH:] + dot(w_ref[1], v_ref[0 : SEQ * OWN], NT)
     weight = weight * (1.0 / (PANEL * math.sqrt(CORES * ZED * SEQ * PANEL)))
+    group = lax.div(lax.broadcasted_iota(jnp.int32, (2 * OWN, CH), 1), OWN)
+    line = lax.broadcasted_iota(jnp.int32, (2 * OWN, CH), 0)
+
+    @pl.when(me > 0)
+    def _():
+        pl.semaphore_wait(vouch_sem, 1)
+
+    for i, place in enumerate(EARLY):
+        turned = pltpu.roll(weight[place * OWN : (place + 1) * OWN], 0, 1, stride=OWN, stride_axis=0)
+        row = jnp.sum(jnp.where(group[:OWN] == line[:OWN], turned, 0.0), axis=0, keepdims=True)
+        early_row[i : i + 1] = row
+        here = early & (dp == place)
+
+        @pl.when(here)
+        def _():
+            recv_early[pl.ds(dp * SEQ + me, 1)] = row
+
+        @pl.when(jnp.logical_not(here))
+        def _():
+            send(
+                early_row.at[pl.ds(i, 1)], recv_early.at[pl.ds(dp * SEQ + me, 1)], 6,
+                {"seq": 0, "dp": place},
+            )
+
     weight = weight.reshape(ZED, CORES, OWN, CH)
     for side in range(CORES):
         part[side] = weight[:, side]
@@ -192,7 +242,10 @@
     await_bytes(recv_z.at[pl.ds(0, ZED - 1)], recv_sem, 3)
     own_sum[...] = jnp.sum(recv_z[...], axis=0)
     for peer in seq_peers:
-        send(own_sum, recv_s.at[me], 5, {"seq": peer})
+        @pl.when(jnp.logical_not(early_dp & (peer == 0)))
+        def _():
+            send(own_sum, recv_s.at[me], 5, {"seq": peer})
+
     recv_s[me] = own_sum[...]
 
     await_bytes(recv_in.at[pl.ds(0, SEQ - 1)], recv_sem, 4)
@@ -200,27 +253,60 @@
         block = recv_in[...].astype(F32)[:, h * OWN : (h + 1) * OWN].reshape(CH, HALF)
         in_ref[0, h * HALF : (h + 1) * HALF] = block.T.astype(BF16)
 
-    await_bytes(recv_s.at[pl.ds(0, SEQ - 1)], recv_sem, 5)
-    group = lax.div(lax.broadcasted_iota(jnp.int32, (OWN, CH), 1), OWN)
-    result = jnp.zeros((OWN, CH), F32)
-    for s in range(SEQ):
-        turned = pltpu.roll(recv_s[s], lax.rem(s + SEQ - me, SEQ) * OWN, 1)
-        result = jnp.where(group == s, turned, result)
-    fg_ref[...] = result
+    @pl.when(jnp.logical_not(early))
+    def _():
+        await_bytes(recv_s.at[pl.ds(0, SEQ - 1)], recv_sem, 5)
+        result = jnp.zeros((OWN, CH), F32)
+        for s in range(SEQ):
+            turned = pltpu.roll(recv_s[s], lax.rem(s + SEQ - me, SEQ) * OWN, 1)
+            result = jnp.where(group[:OWN] == s, turned, result)
+        fg_ref[...] = result
+
+    @pl.when(early)
+    def _():
+        await_bytes(recv_early.at[pl.ds(0, SEQ * CORES * ZED - 1)], recv_sem, 6)
+        total = jnp.sum(recv_early[...].reshape(CORES * ZED, SEQ, CH), axis=0)
+        turned = pltpu.roll(total, 0, 1, stride=OWN, stride_axis=0)
+        for r in range(OWN):
+            shifted = turned if r == 0 else pltpu.roll(turned, CH - r * OWN, 1)
+            fg_ref[r : r + 1] = jnp.sum(jnp.where(group == line, shifted, 0.0), axis=0, keepdims=True)
 
     await_bytes(send_ug.at[pl.ds(0, SEQ - 1)], send_sem, 0)
     await_bytes(send_f.at[pl.ds(0, SEQ - 1)], send_sem, 1)
     await_bytes(from_core, send_sem, 2)
     await_bytes(pair_sum.at[pl.ds(0, ZED - 1)], send_sem, 3)
     await_bytes(send_in.at[pl.ds(0, SEQ - 1)], send_sem, 4)
-    await_bytes(recv_s.at[pl.ds(0, SEQ - 1)], send_sem, 5)
+    sent = jnp.where(early_dp & (me > 0), SEQ - 2, SEQ - 1)
+
+    def sent_one(i, carry):
+        await_bytes(own_sum, send_sem, 5)
+        return carry
+
+    lax.fori_loop(0, sent, sent_one, 0)
+    if len(EARLY) > 1:
+        await_bytes(early_row.at[pl.ds(0, len(EARLY) - 1)], send_sem, 6)
+
+    @pl.when(jnp.logical_not(early))
+    def _():
+        await_bytes(early_row.at[pl.ds(0, 1)], send_sem, 6)
+
+
+def place(in_vmem, fg_vmem, in_hbm, fg_hbm, sem):
+    copies = [
+        pltpu.make_async_copy(in_vmem, in_hbm, sem.at[0]),
+        pltpu.make_async_copy(fg_vmem, fg_hbm, sem.at[1]),
+    ]
+    for copy in copies:
+        copy.start()
+    for copy in copies:
+        copy.wait()
 
 
 def on_device(signal, out_grad, filt, skip):
     vmem = pl.BlockSpec(memory_space=pltpu.VMEM)
     operands = (signal, out_grad, filt, skip.reshape(1, CH), jnp.asarray(table()))
     tiles = (SEQ, 2, 2 * OWN, HALF)
-    return pl.pallas_call(
+    grads = pl.pallas_call(
         kernel,
         out_shape=(
             pltpu.VMEM((1, PANEL, CH), BF16),
@@ -250,15 +336,29 @@
             pltpu.VMEM((SEQ, OWN, CH), F32),
             pltpu.VMEM((SEQ, 2 * OWN, HALF), BF16),
             pltpu.VMEM((SEQ, 2 * OWN, HALF), BF16),
-            pltpu.SemaphoreType.DMA((6,)),
-            pltpu.SemaphoreType.DMA((6,)),
+            pltpu.SemaphoreType.DMA((7,)),
+            pltpu.SemaphoreType.DMA((7,)),
             pltpu.SemaphoreType.DMA((5,)),
             pltpu.SemaphoreType.REGULAR,
+            pltpu.SemaphoreType.REGULAR,
+            pltpu.VMEM((OWN, CH), F32),
+            pltpu.VMEM((SEQ * CORES * ZED, CH), F32),
         ],
         compiler_params=pltpu.CompilerParams(
             collective_id=0, has_side_effects=True, vmem_limit_bytes=16 * 1024 * 1024
         ),
     )(*(pltpu.with_memory_space_constraint(x, pltpu.HBM) for x in operands))
+    return pl.pallas_call(
+        place,
+        out_shape=(
+            jax.ShapeDtypeStruct((1, PANEL, CH), BF16),
+            jax.ShapeDtypeStruct((OWN, CH), F32),
+        ),
+        in_specs=[vmem] * 2,
+        out_specs=(pl.BlockSpec(memory_space=pltpu.HBM),) * 2,
+        scratch_shapes=[pltpu.SemaphoreType.DMA((2,))],
+        compiler_params=pltpu.CompilerParams(vmem_limit_bytes=1024 * 1024),
+    )(*grads)
 
 
 def solution(mesh):

time: 36.4 us -> 34.6 us (0.951)
  the two profiles are of different devices: /device:TPU:1 before, /device:TPU:8 now
where the time goes in v2:
time: 34.6 us; the launch traced here: 34.4 us
  Pallas kernels  33.8 us (98%)
  between operations  0.64 us (2%)
    pallas_call x1, Pallas kernels, on_device(): pl.pallas_call(kernel, out_shape=(pltpu.VMEM((1, PANEL, CH), BF16), pltpu...  33.1 us

profile of v2, /device:TPU:8, one launch (start us, length us, event | category | flops | bytes accessed | tf_op | source)
XLA Modules:
  0.0 34.4 jit_solution(18300304329860880901)
XLA Ops:
  0.6 33.1 %shard_map.68 = (bf16[1,256,128]{2,1,0:T(8,128)(2,1)S(1)}, f32[8,128]{1,0:T(8,128)S(1)}) custom-call(bf16[1,256,128]{2,1,0:T(8,128)(2,1)} %u_hbm.1, bf16[1,256,128]{2,1,0:T(8,128)(2,1)} %g_hbm.1, f32[256,128]{1,0:T(8,128)} %f_hbm.1, f32[1,128]{1,0:T(1,128)} %bitcast.1, bf16[2,256,512]{2,1,0:T(8,128)(2,1)} %constant.2.clone.w_hbm), custom_call_target="tpu_custom_call" | custom-call | tf_op jit(solution)/shard_map/pallas_call | solution.py:309
  33.8 0.7 %shard_map.69 = (bf16[1,256,128]{2,1,0:T(8,128)(2,1)}, f32[8,128]{1,0:T(8,128)}) custom-call(bf16[1,256,128]{2,1,0:T(8,128)(2,1)S(1)} %get-tuple-element.4.in_vmem, f32[8,128]{1,0:T(8,128)S(1)} %get-tuple-element.5.fg_vmem), custom_call_target="tpu_custom_call" | custom-call | tf_op jit(solution)/shard_map/pallas_call | solution.py:351

commit v3 on v2

--- a/solution.py
+++ b/solution.py
@@ -19,6 +19,7 @@
     ((i, j) for i in range(4) for j in range(4) if i + j), key=lambda o: -sum(min(k, 4 - k) for k in o)
 )
 Z_OFFSETS = sorted(range(1, ZED), key=lambda k: -min(k, ZED - k))
+FAR, NEARER = Z_OFFSETS[:3], Z_OFFSETS[3:]
 F32, BF16 = jnp.float32, jnp.bfloat16
 NT = (((1,), (1,)), ((), ()))
 NN = (((1,), (0,)), ((), ()))
@@ -71,7 +72,7 @@
 def kernel(
     u_hbm, g_hbm, f_hbm, skip_hbm, w_hbm, in_ref, fg_ref,
     u_ref, g_ref, f_ref, skip_ref, w_ref, send_ug, recv_ug, send_f, recv_f, spec, spec_f, spin, v_ref, part, from_core, pair_sum, recv_z,
-    own_sum, recv_s, send_in, recv_in, send_sem, recv_sem, load_sem, relay_sem, vouch_sem, early_row, recv_early,
+    own_sum, recv_s, send_in, recv_in, send_sem, recv_sem, load_sem, relay_sem, vouch_sem, pair_sem, recv_far, early_row, recv_early,
 ):
     me, dp = lax.axis_index("seq"), lax.axis_index("dp")
     z, core = lax.div(dp, CORES), lax.rem(dp, CORES)
@@ -158,6 +159,12 @@
     recv_f[me] = send_f[me]
 
     loads[4].wait()
+    pl.semaphore_wait(relay_sem, 2)
+    pl.semaphore_signal(pair_sem, inc=1, device_id={"dp": z * CORES + other})
+
+    @pl.when(me > 0)
+    def _():
+        pl.semaphore_wait(vouch_sem, 1)
 
     def transform(tiles_ref):
         lhs = jnp.concatenate(
@@ -189,10 +196,6 @@
     group = lax.div(lax.broadcasted_iota(jnp.int32, (2 * OWN, CH), 1), OWN)
     line = lax.broadcasted_iota(jnp.int32, (2 * OWN, CH), 0)
 
-    @pl.when(me > 0)
-    def _():
-        pl.semaphore_wait(vouch_sem, 1)
-
     for i, place in enumerate(EARLY):
         turned = pltpu.roll(weight[place * OWN : (place + 1) * OWN], 0, 1, stride=OWN, stride_axis=0)
         row = jnp.sum(jnp.where(group[:OWN] == line[:OWN], turned, 0.0), axis=0, keepdims=True)
@@ -210,9 +213,14 @@
                 {"seq": 0, "dp": place},
             )
 
-    weight = weight.reshape(ZED, CORES, OWN, CH)
+    blocks = weight.reshape(ZED, CORES, OWN, CH)
     for side in range(CORES):
-        part[side] = weight[:, side]
+        part[side] = blocks[:, side]
+    pl.semaphore_wait(pair_sem, 1)
+    for i, k in enumerate(FAR):
+        peer = z_peer(k)
+        for side in range(CORES):
+            send(part.at[side, peer], recv_far.at[i, core], 7, {"dp": peer * CORES + side})
     send(part.at[other], from_core, 2, {"dp": z * CORES + other})
 
     await_bytes(recv_f.at[pl.ds(0, SEQ - 1)], recv_sem, 1)
@@ -221,11 +229,9 @@
 
     await_bytes(from_core, recv_sem, 2)
     pair_sum[...] = part[core] + from_core[...]
-    pl.semaphore_wait(relay_sem, 2)
-    for k in Z_OFFSETS:
+    for i, k in enumerate(NEARER):
         peer = z_peer(k)
-        send(pair_sum.at[peer], recv_z.at[z], 3, {"dp": peer * CORES + core})
-    recv_z[z] = pair_sum[z]
+        send(pair_sum.at[peer], recv_z.at[i], 3, {"dp": peer * CORES + core})
 
     correlate(
         lambda a, lane: (spec_f[a, :, lane : lane + HALF], spec_f[a, :, FREQ + lane : FREQ + lane + HALF]),
@@ -239,11 +245,20 @@
         send(send_in.at[peer], recv_in.at[me], 4, {"seq": peer})
     recv_in[me] = send_in[me]
 
-    await_bytes(recv_z.at[pl.ds(0, ZED - 1)], recv_sem, 3)
-    own_sum[...] = jnp.sum(recv_z[...], axis=0)
-    for peer in seq_peers:
-        @pl.when(jnp.logical_not(early_dp & (peer == 0)))
-        def _():
+    await_bytes(recv_z, recv_sem, 3)
+    await_bytes(recv_far, recv_sem, 7)
+    far = recv_far[...].reshape(len(FAR) * CORES, OWN, CH)
+    own_sum[...] = jnp.sum(recv_z[...], axis=0) + jnp.sum(far, axis=0) + pair_sum[z]
+    @pl.when(early_dp)
+    def _():
+        for peer in seq_peers:
+            @pl.when(peer > 0)
+            def _():
+                send(own_sum, recv_s.at[me], 5, {"seq": peer})
+
+    @pl.when(jnp.logical_not(early_dp))
+    def _():
+        for peer in seq_peers:
             send(own_sum, recv_s.at[me], 5, {"seq": peer})
 
     recv_s[me] = own_sum[...]
@@ -252,6 +267,29 @@
     for h in range(2):
         block = recv_in[...].astype(F32)[:, h * OWN : (h + 1) * OWN].reshape(CH, HALF)
         in_ref[0, h * HALF : (h + 1) * HALF] = block.T.astype(BF16)
+
+    await_bytes(send_ug.at[pl.ds(0, SEQ - 1)], send_sem, 0)
+    await_bytes(send_f.at[pl.ds(0, SEQ - 1)], send_sem, 1)
+    await_bytes(from_core, send_sem, 2)
+    await_bytes(recv_z, send_sem, 3)
+    await_bytes(recv_far, send_sem, 7)
+    await_bytes(send_in.at[pl.ds(0, SEQ - 1)], send_sem, 4)
+    fewer = early_dp & (me > 0)
+
+    @pl.when(fewer)
+    def _():
+        await_bytes(recv_s.at[pl.ds(0, SEQ - 2)], send_sem, 5)
+
+    @pl.when(jnp.logical_not(fewer))
+    def _():
+        await_bytes(recv_s.at[pl.ds(0, SEQ - 1)], send_sem, 5)
+
+    if len(EARLY) > 1:
+        await_bytes(early_row.at[pl.ds(0, len(EARLY) - 1)], send_sem, 6)
+
+    @pl.when(jnp.logical_not(early))
+    def _():
+        await_bytes(early_row.at[pl.ds(0, 1)], send_sem, 6)
 
     @pl.when(jnp.logical_not(early))
     def _():
@@ -270,25 +308,6 @@
         for r in range(OWN):
             shifted = turned if r == 0 else pltpu.roll(turned, CH - r * OWN, 1)
             fg_ref[r : r + 1] = jnp.sum(jnp.where(group == line, shifted, 0.0), axis=0, keepdims=True)
-
-    await_bytes(send_ug.at[pl.ds(0, SEQ - 1)], send_sem, 0)
-    await_bytes(send_f.at[pl.ds(0, SEQ - 1)], send_sem, 1)
-    await_bytes(from_core, send_sem, 2)
-    await_bytes(pair_sum.at[pl.ds(0, ZED - 1)], send_sem, 3)
-    await_bytes(send_in.at[pl.ds(0, SEQ - 1)], send_sem, 4)
-    sent = jnp.where(early_dp & (me > 0), SEQ - 2, SEQ - 1)
-
-    def sent_one(i, carry):
-        await_bytes(own_sum, send_sem, 5)
-        return carry
-
-    lax.fori_loop(0, sent, sent_one, 0)
-    if len(EARLY) > 1:
-        await_bytes(early_row.at[pl.ds(0, len(EARLY) - 1)], send_sem, 6)
-
-    @pl.when(jnp.logical_not(early))
-    def _():
-        await_bytes(early_row.at[pl.ds(0, 1)], send_sem, 6)
 
 
 def place(in_vmem, fg_vmem, in_hbm, fg_hbm, sem):
@@ -331,16 +350,18 @@
             pltpu.VMEM((CORES, ZED, OWN, CH), F32),
             pltpu.VMEM((ZED, OWN, CH), F32),
             pltpu.VMEM((ZED, OWN, CH), F32),
-            pltpu.VMEM((ZED, OWN, CH), F32),
+            pltpu.VMEM((len(NEARER), OWN, CH), F32),
             pltpu.VMEM((OWN, CH), F32),
             pltpu.VMEM((SEQ, OWN, CH), F32),
             pltpu.VMEM((SEQ, 2 * OWN, HALF), BF16),
             pltpu.VMEM((SEQ, 2 * OWN, HALF), BF16),
-            pltpu.SemaphoreType.DMA((7,)),
-            pltpu.SemaphoreType.DMA((7,)),
+            pltpu.SemaphoreType.DMA((8,)),
+            pltpu.SemaphoreType.DMA((8,)),
             pltpu.SemaphoreType.DMA((5,)),
             pltpu.SemaphoreType.REGULAR,
             pltpu.SemaphoreType.REGULAR,
+            pltpu.SemaphoreType.REGULAR,
+            pltpu.VMEM((len(FAR), CORES, OWN, CH), F32),
             pltpu.VMEM((OWN, CH), F32),
             pltpu.VMEM((SEQ * CORES * ZED, CH), F32),
         ],

time: 34.6 us -> 34 us (0.983)
  the two profiles are of different devices: /device:TPU:8 before, /device:TPU:2 now
where the time goes in v3:
time: 34 us; the launch traced here: 33.9 us
  Pallas kernels  33.2 us (98%)
  between operations  0.64 us (2%)
    pallas_call x1, Pallas kernels, on_device(): pl.pallas_call(kernel, out_shape=(pltpu.VMEM((1, PANEL, CH), BF16), pltpu...  32.6 us

profile of v3, /device:TPU:2, one launch (start us, length us, event | category | flops | bytes accessed | tf_op | source)
XLA Modules:
  0.0 33.9 jit_solution(1448058950740311326)
XLA Ops:
  0.6 32.6 %shard_map.68 = (bf16[1,256,128]{2,1,0:T(8,128)(2,1)S(1)}, f32[8,128]{1,0:T(8,128)S(1)}) custom-call(bf16[1,256,128]{2,1,0:T(8,128)(2,1)} %u_hbm.1, bf16[1,256,128]{2,1,0:T(8,128)(2,1)} %g_hbm.1, f32[256,128]{1,0:T(8,128)} %f_hbm.1, f32[1,128]{1,0:T(1,128)} %bitcast.1, bf16[2,256,512]{2,1,0:T(8,128)(2,1)} %constant.2.clone.w_hbm), custom_call_target="tpu_custom_call" | custom-call | tf_op jit(solution)/shard_map/pallas_call | solution.py:328
  33.2 0.7 %shard_map.69 = (bf16[1,256,128]{2,1,0:T(8,128)(2,1)}, f32[8,128]{1,0:T(8,128)}) custom-call(bf16[1,256,128]{2,1,0:T(8,128)(2,1)S(1)} %get-tuple-element.4.in_vmem, f32[8,128]{1,0:T(8,128)S(1)} %get-tuple-element.5.fg_vmem), custom_call_target="tpu_custom_call" | custom-call | tf_op jit(solution)/shard_map/pallas_call | solution.py:372

commit v4 on v3

--- a/solution.py
+++ b/solution.py
@@ -14,7 +14,8 @@
 PANEL, HALF, CH, OWN = 256, 128, 128, 8
 FREQ = PANEL
 NEAR = 4
-EARLY = (1,)
+EARLY = ((0, 1), (1, 0), (4, 0), (1, 1), (4, 1), (0, 2), (0, 3))
+COLUMNS = sorted({seq for seq, _ in EARLY})
 SEQ_OFFSETS = sorted(
     ((i, j) for i in range(4) for j in range(4) if i + j), key=lambda o: -sum(min(k, 4 - k) for k in o)
 )
@@ -99,16 +100,16 @@
     for load in loads[2:]:
         load.start()
 
-    early_dp = (dp >= EARLY[0]) & (dp <= EARLY[-1])
-    early = (me == 0) & early_dp
-
+    any_of = lambda terms: functools.reduce(jnp.logical_or, terms)
+    early = any_of([(me == seq) & (dp == place) for seq, place in EARLY])
+    early_dp = any_of([dp == place for place in sorted({place for _, place in EARLY})])
+    in_column = any_of([me == seq for seq in COLUMNS])
     greetings = SEQ + 2 * NEAR
-    for place in EARLY:
+    for seq, place in EARLY:
         strangers = [k for k in range(CORES * ZED) if not beside(k, place)]
-        unknown = functools.reduce(jnp.logical_or, [dp == k for k in strangers])
-        greetings += jnp.where((me == 0) & unknown, 1, 0)
-
-        @pl.when((me == 0) & (dp == place))
+        greetings += jnp.where((me == seq) & any_of([dp == k for k in strangers]), 1, 0)
+
+        @pl.when((me == seq) & (dp == place))
         def _():
             for k in strangers:
                 pl.semaphore_signal(barrier, inc=1, device_id={"dp": k})
@@ -146,7 +147,7 @@
     for k in (NEAR, ZED - NEAR):
         pl.semaphore_signal(relay_sem, inc=1, device_id={"dp": z_peer(k) * CORES + core})
 
-    @pl.when(me == 0)
+    @pl.when(in_column)
     def _():
         for peer in seq_peers:
             pl.semaphore_signal(vouch_sem, inc=1, device_id={"seq": peer})
@@ -162,9 +163,7 @@
     pl.semaphore_wait(relay_sem, 2)
     pl.semaphore_signal(pair_sem, inc=1, device_id={"dp": z * CORES + other})
 
-    @pl.when(me > 0)
-    def _():
-        pl.semaphore_wait(vouch_sem, 1)
+    pl.semaphore_wait(vouch_sem, jnp.where(in_column, len(COLUMNS) - 1, len(COLUMNS)))
 
     def transform(tiles_ref):
         lhs = jnp.concatenate(
@@ -196,11 +195,12 @@
     group = lax.div(lax.broadcasted_iota(jnp.int32, (2 * OWN, CH), 1), OWN)
     line = lax.broadcasted_iota(jnp.int32, (2 * OWN, CH), 0)
 
-    for i, place in enumerate(EARLY):
+    for i, (seq, place) in enumerate(EARLY):
         turned = pltpu.roll(weight[place * OWN : (place + 1) * OWN], 0, 1, stride=OWN, stride_axis=0)
-        row = jnp.sum(jnp.where(group[:OWN] == line[:OWN], turned, 0.0), axis=0, keepdims=True)
+        place_of = lax.rem(line[:OWN] + seq, SEQ)
+        row = jnp.sum(jnp.where(group[:OWN] == place_of, turned, 0.0), axis=0, keepdims=True)
         early_row[i : i + 1] = row
-        here = early & (dp == place)
+        here = (me == seq) & (dp == place)
 
         @pl.when(here)
         def _():
@@ -210,7 +210,7 @@
         def _():
             send(
                 early_row.at[pl.ds(i, 1)], recv_early.at[pl.ds(dp * SEQ + me, 1)], 6,
-                {"seq": 0, "dp": place},
+                {"seq": seq, "dp": place},
             )
 
     blocks = weight.reshape(ZED, CORES, OWN, CH)
@@ -252,7 +252,9 @@
     @pl.when(early_dp)
     def _():
         for peer in seq_peers:
-            @pl.when(peer > 0)
+            direct = any_of([(peer == seq) & (dp == place) for seq, place in EARLY])
+
+            @pl.when(jnp.logical_not(direct))
             def _():
                 send(own_sum, recv_s.at[me], 5, {"seq": peer})
 
@@ -274,22 +276,19 @@
     await_bytes(recv_z, send_sem, 3)
     await_bytes(recv_far, send_sem, 7)
     await_bytes(send_in.at[pl.ds(0, SEQ - 1)], send_sem, 4)
-    fewer = early_dp & (me > 0)
-
-    @pl.when(fewer)
-    def _():
-        await_bytes(recv_s.at[pl.ds(0, SEQ - 2)], send_sem, 5)
-
-    @pl.when(jnp.logical_not(fewer))
-    def _():
-        await_bytes(recv_s.at[pl.ds(0, SEQ - 1)], send_sem, 5)
-
-    if len(EARLY) > 1:
-        await_bytes(early_row.at[pl.ds(0, len(EARLY) - 1)], send_sem, 6)
-
-    @pl.when(jnp.logical_not(early))
-    def _():
-        await_bytes(early_row.at[pl.ds(0, 1)], send_sem, 6)
+    sent = SEQ - 1
+    for seq, place in EARLY:
+        sent -= jnp.where((dp == place) & (me != seq), 1, 0)
+
+    def sent_one(i, carry):
+        await_bytes(own_sum, send_sem, 5)
+        return carry
+
+    lax.fori_loop(0, sent, sent_one, 0)
+    for seq, place in EARLY:
+        @pl.when(jnp.logical_not((me == seq) & (dp == place)))
+        def _():
+            await_bytes(early_row.at[pl.ds(0, 1)], send_sem, 6)
 
     @pl.when(jnp.logical_not(early))
     def _():
@@ -304,6 +303,7 @@
     def _():
         await_bytes(recv_early.at[pl.ds(0, SEQ * CORES * ZED - 1)], recv_sem, 6)
         total = jnp.sum(recv_early[...].reshape(CORES * ZED, SEQ, CH), axis=0)
+        total = pltpu.roll(total, (SEQ - me) * OWN, 1)
         turned = pltpu.roll(total, 0, 1, stride=OWN, stride_axis=0)
         for r in range(OWN):
             shifted = turned if r == 0 else pltpu.roll(turned, CH - r * OWN, 1)
@@ -362,7 +362,7 @@
             pltpu.SemaphoreType.REGULAR,
             pltpu.SemaphoreType.REGULAR,
             pltpu.VMEM((len(FAR), CORES, OWN, CH), F32),
-            pltpu.VMEM((OWN, CH), F32),
+            pltpu.VMEM((2 * OWN, CH), F32),
             pltpu.VMEM((SEQ * CORES * ZED, CH), F32),
         ],
         compiler_params=pltpu.CompilerParams(

time: 34 us -> 33.5 us (0.985)
  the two profiles are of different devices: /device:TPU:2 before, /device:TPU:6 now
where the time goes in v4:
time: 33.5 us; the launch traced here: 33.3 us
  Pallas kernels  32.7 us (98%)
  between operations  0.64 us (2%)
    pallas_call x1, Pallas kernels, on_device(): pl.pallas_call(kernel, out_shape=(pltpu.VMEM((1, PANEL, CH), BF16), pltpu...  32 us

profile of v4, /device:TPU:6, one launch (start us, length us, event | category | flops | bytes accessed | tf_op | source)
XLA Modules:
  0.0 33.3 jit_solution(8768413158345516939)
XLA Ops:
  0.6 32.0 %shard_map.68 = (bf16[1,256,128]{2,1,0:T(8,128)(2,1)S(1)}, f32[8,128]{1,0:T(8,128)S(1)}) custom-call(bf16[1,256,128]{2,1,0:T(8,128)(2,1)} %u_hbm.1, bf16[1,256,128]{2,1,0:T(8,128)(2,1)} %g_hbm.1, f32[256,128]{1,0:T(8,128)} %f_hbm.1, f32[1,128]{1,0:T(1,128)} %bitcast.1, bf16[2,256,512]{2,1,0:T(8,128)(2,1)} %constant.2.clone.w_hbm), custom_call_target="tpu_custom_call" | custom-call | tf_op jit(solution)/shard_map/pallas_call | solution.py:328
  32.6 0.7 %shard_map.69 = (bf16[1,256,128]{2,1,0:T(8,128)(2,1)}, f32[8,128]{1,0:T(8,128)}) custom-call(bf16[1,256,128]{2,1,0:T(8,128)(2,1)S(1)} %get-tuple-element.4.in_vmem, f32[8,128]{1,0:T(8,128)S(1)} %get-tuple-element.5.fg_vmem), custom_call_target="tpu_custom_call" | custom-call | tf_op jit(solution)/shard_map/pallas_call | solution.py:372

commit v5 on v4

--- a/solution.py
+++ b/solution.py
@@ -14,7 +14,7 @@
 PANEL, HALF, CH, OWN = 256, 128, 128, 8
 FREQ = PANEL
 NEAR = 4
-EARLY = ((0, 1), (1, 0), (4, 0), (1, 1), (4, 1), (0, 2), (0, 3))
+EARLY = ((0, 1), (1, 0), (4, 0), (1, 1), (4, 1), (0, 2), (0, 3), (8, 0), (8, 1), (12, 0), (12, 1))
 COLUMNS = sorted({seq for seq, _ in EARLY})
 SEQ_OFFSETS = sorted(
     ((i, j) for i in range(4) for j in range(4) if i + j), key=lambda o: -sum(min(k, 4 - k) for k in o)
@@ -195,7 +195,8 @@
     group = lax.div(lax.broadcasted_iota(jnp.int32, (2 * OWN, CH), 1), OWN)
     line = lax.broadcasted_iota(jnp.int32, (2 * OWN, CH), 0)
 
-    for i, (seq, place) in enumerate(EARLY):
+    def tell(i):
+        seq, place = EARLY[i]
         turned = pltpu.roll(weight[place * OWN : (place + 1) * OWN], 0, 1, stride=OWN, stride_axis=0)
         place_of = lax.rem(line[:OWN] + seq, SEQ)
         row = jnp.sum(jnp.where(group[:OWN] == place_of, turned, 0.0), axis=0, keepdims=True)
@@ -213,6 +214,7 @@
                 {"seq": seq, "dp": place},
             )
 
+    tell(0)
     blocks = weight.reshape(ZED, CORES, OWN, CH)
     for side in range(CORES):
         part[side] = blocks[:, side]
@@ -222,6 +224,8 @@
         for side in range(CORES):
             send(part.at[side, peer], recv_far.at[i, core], 7, {"dp": peer * CORES + side})
     send(part.at[other], from_core, 2, {"dp": z * CORES + other})
+    for i in range(1, len(EARLY)):
+        tell(i)
 
     await_bytes(recv_f.at[pl.ds(0, SEQ - 1)], recv_sem, 1)
     both = transform(recv_f).reshape(SEQ, 2, OWN, 2 * FREQ)
@@ -362,7 +366,7 @@
             pltpu.SemaphoreType.REGULAR,
             pltpu.SemaphoreType.REGULAR,
             pltpu.VMEM((len(FAR), CORES, OWN, CH), F32),
-            pltpu.VMEM((2 * OWN, CH), F32),
+            pltpu.VMEM((4 * OWN, CH), F32),
             pltpu.VMEM((SEQ * CORES * ZED, CH), F32),
         ],
         compiler_params=pltpu.CompilerParams(

time: 33.5 us -> 33.2 us (level)
  the two profiles are of different devices: /device:TPU:6 before, /device:TPU:1 now
where the time goes in v5:
time: 33.2 us; the launch traced here: 32.7 us
  Pallas kernels  32.1 us (97%)
  between operations  0.64 us (2%)
    pallas_call x1, Pallas kernels, on_device(): pl.pallas_call(kernel, out_shape=(pltpu.VMEM((1, PANEL, CH), BF16), pltpu...  31.4 us

profile of v5, /device:TPU:1, one launch (start us, length us, event | category | flops | bytes accessed | tf_op | source)
XLA Modules:
  0.0 32.7 jit_solution(1316183786017178550)
XLA Ops:
  0.6 31.4 %shard_map.68 = (bf16[1,256,128]{2,1,0:T(8,128)(2,1)S(1)}, f32[8,128]{1,0:T(8,128)S(1)}) custom-call(bf16[1,256,128]{2,1,0:T(8,128)(2,1)} %u_hbm.1, bf16[1,256,128]{2,1,0:T(8,128)(2,1)} %g_hbm.1, f32[256,128]{1,0:T(8,128)} %f_hbm.1, f32[1,128]{1,0:T(1,128)} %bitcast.1, bf16[2,256,512]{2,1,0:T(8,128)(2,1)} %constant.2.clone.w_hbm), custom_call_target="tpu_custom_call" | custom-call | tf_op jit(solution)/shard_map/pallas_call | solution.py:332
  32.0 0.7 %shard_map.69 = (bf16[1,256,128]{2,1,0:T(8,128)(2,1)}, f32[8,128]{1,0:T(8,128)}) custom-call(bf16[1,256,128]{2,1,0:T(8,128)(2,1)S(1)} %get-tuple-element.4.in_vmem, f32[8,128]{1,0:T(8,128)S(1)} %get-tuple-element.5.fg_vmem), custom_call_target="tpu_custom_call" | custom-call | tf_op jit(solution)/shard_map/pallas_call | solution.py:376

commit v6 on v5

--- a/solution.py
+++ b/solution.py
@@ -14,7 +14,7 @@
 PANEL, HALF, CH, OWN = 256, 128, 128, 8
 FREQ = PANEL
 NEAR = 4
-EARLY = ((0, 1), (1, 0), (4, 0), (1, 1), (4, 1), (0, 2), (0, 3), (8, 0), (8, 1), (12, 0), (12, 1))
+EARLY = ((0, 1), (1, 0), (4, 0), (1, 1), (4, 1), (0, 2), (0, 3), (8, 0), (8, 1), (12, 0), (12, 1), (2, 0), (2, 1), (5, 0), (5, 1), (3, 0), (3, 1))
 COLUMNS = sorted({seq for seq, _ in EARLY})
 SEQ_OFFSETS = sorted(
     ((i, j) for i in range(4) for j in range(4) if i + j), key=lambda o: -sum(min(k, 4 - k) for k in o)

time: 33.2 us -> 33.2 us (level)
  no operation moved by 1% of the time
where the time goes in v6:
time: 33.2 us; the launch traced here: 32.7 us
  Pallas kernels  32.1 us (97%)
  between operations  0.64 us (2%)
    pallas_call x1, Pallas kernels, on_device(): pl.pallas_call(kernel, out_shape=(pltpu.VMEM((1, PANEL, CH), BF16), pltpu...  31.4 us

profile of v6, /device:TPU:1, one launch (start us, length us, event | category | flops | bytes accessed | tf_op | source)
XLA Modules:
  0.0 32.7 jit_solution(4434953109174746152)
XLA Ops:
  0.6 31.4 %shard_map.68 = (bf16[1,256,128]{2,1,0:T(8,128)(2,1)S(1)}, f32[8,128]{1,0:T(8,128)S(1)}) custom-call(bf16[1,256,128]{2,1,0:T(8,128)(2,1)} %u_hbm.1, bf16[1,256,128]{2,1,0:T(8,128)(2,1)} %g_hbm.1, f32[256,128]{1,0:T(8,128)} %f_hbm.1, f32[1,128]{1,0:T(1,128)} %bitcast.1, bf16[2,256,512]{2,1,0:T(8,128)(2,1)} %constant.2.clone.w_hbm), custom_call_target="tpu_custom_call" | custom-call | tf_op jit(solution)/shard_map/pallas_call | solution.py:332
  32.1 0.7 %shard_map.69 = (bf16[1,256,128]{2,1,0:T(8,128)(2,1)}, f32[8,128]{1,0:T(8,128)}) custom-call(bf16[1,256,128]{2,1,0:T(8,128)(2,1)S(1)} %get-tuple-element.4.in_vmem, f32[8,128]{1,0:T(8,128)S(1)} %get-tuple-element.5.fg_vmem), custom_call_target="tpu_custom_call" | custom-call | tf_op jit(solution)/shard_map/pallas_call | solution.py:376

commit v7 on v6

--- a/solution.py
+++ b/solution.py
@@ -88,13 +88,13 @@
             ((u_hbm, u_ref), (g_hbm, g_ref), (f_hbm, f_ref), (skip_hbm, skip_ref), (w_hbm, w_ref))
         )
     ]
+    barrier = pltpu.get_barrier_semaphore()
+    for peer in seq_peers:
+        pl.semaphore_signal(barrier, inc=1, device_id={"seq": peer})
+    for k in Z_OFFSETS[-2 * NEAR :]:
+        pl.semaphore_signal(barrier, inc=1, device_id={"dp": z_peer(k) * CORES + core})
     for load in loads[:2]:
         load.start()
-    barrier = pltpu.get_barrier_semaphore()
-    for k in Z_OFFSETS[-2 * NEAR :]:
-        pl.semaphore_signal(barrier, inc=1, device_id={"dp": z_peer(k) * CORES + core})
-    for peer in seq_peers:
-        pl.semaphore_signal(barrier, inc=1, device_id={"seq": peer})
     pl.semaphore_signal(barrier, inc=1, device_id={"dp": z * CORES + other})
 
     for load in loads[2:]:

time: 33.2 us -> 33.3 us (level)
  no operation moved by 1% of the time
where the time goes in v7:
time: 33.3 us; the launch traced here: 32.6 us
  Pallas kernels  32 us (96%)
  between operations  0.64 us (2%)
    pallas_call x1, Pallas kernels, on_device(): pl.pallas_call(kernel, out_shape=(pltpu.VMEM((1, PANEL, CH), BF16), pltpu...  31.3 us

profile of v7, /device:TPU:1, one launch (start us, length us, event | category | flops | bytes accessed | tf_op | source)
XLA Modules:
  0.0 32.6 jit_solution(2507513049817509229)
XLA Ops:
  0.6 31.3 %shard_map.68 = (bf16[1,256,128]{2,1,0:T(8,128)(2,1)S(1)}, f32[8,128]{1,0:T(8,128)S(1)}) custom-call(bf16[1,256,128]{2,1,0:T(8,128)(2,1)} %u_hbm.1, bf16[1,256,128]{2,1,0:T(8,128)(2,1)} %g_hbm.1, f32[256,128]{1,0:T(8,128)} %f_hbm.1, f32[1,128]{1,0:T(1,128)} %bitcast.1, bf16[2,256,512]{2,1,0:T(8,128)(2,1)} %constant.2.clone.w_hbm), custom_call_target="tpu_custom_call" | custom-call | tf_op jit(solution)/shard_map/pallas_call | solution.py:332
  32.0 0.7 %shard_map.69 = (bf16[1,256,128]{2,1,0:T(8,128)(2,1)}, f32[8,128]{1,0:T(8,128)}) custom-call(bf16[1,256,128]{2,1,0:T(8,128)(2,1)S(1)} %get-tuple-element.4.in_vmem, f32[8,128]{1,0:T(8,128)S(1)} %get-tuple-element.5.fg_vmem), custom_call_target="tpu_custom_call" | custom-call | tf_op jit(solution)/shard_map/pallas_call | solution.py:376
